TPU v7x, 512 devices: a whole 4x8x8 slice. The times are simulated.
512 devices in a mesh: leaf: 8 (over x, core), sub: 64 (over z, y).
Axes of the slice: x: 4, y: 8, z: 8, core: 2. Of those that a mesh axis runs over, the one named last changes fastest.
Arguments:
- points: bfloat16 [131072, 64], P(('leaf', 'sub')), may hold values from -6 to 6
- omega: bfloat16 [131072, 256], P(('leaf', 'sub')), may hold values from -6 to 6
- samples: float32 [131072, 256], P(('leaf', 'sub')), may hold values from -48 to 48
- ranks: int32 [8, 4], P('leaf'), may hold values from 128 to 256, as said below
- leaf_skeleton: int32 [8, 256], P('leaf'), may hold values from 0 to 16383, as said below
- merge_skeleton: int32 [8, 3, 256], P('leaf'), may hold values from 0 to 511, as said below
Outputs:
- leaf_interp: float32 [131072, 256], P(('leaf', 'sub'))
- node_interp: float32 [8, 3, 512, 256], P('leaf')
- couplings: float32 [8, 3, 256, 256], P('leaf')
- top_compressed: float32 [8, 256, 256], P('leaf')
Inputs may be any that keep to these rules, and one draw needn't show every extreme that they name: ranks[i, l] is the rank of the level-l node holding leaf i (leaves with equal i >> l share it); 256 is reached. `leaf_skeleton`: row i lists 256 distinct point indices within leaf i; the first ranks[i, 0] are its skeleton. merge_skeleton[i, l - 1] lists 256 distinct candidate rows of the level-l node holding leaf i, equal for all its leaves; candidate j < 256 is the lower child's row j, else the upper child's row j - 256; the first ranks[i, l] name rows below the owning child's rank.
All inputs are finite; a program needn't handle non-finite values.
Results may differ from a plain program's by a relative error of at most 0.00076.
Values may be sent and summed in bfloat16 or wider, within the bound.
A program may use at most 128 MiB of HBM per device.

v0:
```python
import jax
import jax.numpy as jnp
from jax import lax
from jax.sharding import PartitionSpec as P

LEVELS = 3


def partner(value, axis, stride):
    mask = 2**stride
    pairs = [(source, source ^ mask) for source in range(lax.axis_size(axis))]
    return lax.ppermute(value, axis, pairs)


def kernel(left, right):
    cross = jnp.einsum("id,jd->ij", left, right, preferred_element_type=jnp.float32)
    left_sq = jnp.sum(jnp.square(left.astype(jnp.float32)), axis=1)
    right_sq = jnp.sum(jnp.square(right.astype(jnp.float32)), axis=1)
    return jnp.exp(-(left_sq[:, None] + right_sq[None, :] - 2.0 * cross) / (0.5 * left.shape[1]))


def factorize(picked):
    gram = jnp.dot(
        picked, picked.T, precision=lax.Precision.HIGHEST, preferred_element_type=jnp.float32
    )
    shift = jnp.sum(picked * picked) / picked.shape[0] + 1e-06
    return jnp.linalg.cholesky(gram + shift * jnp.eye(picked.shape[0], dtype=jnp.float32))


def interpolate(factor, candid, picked):
    right_side = jnp.einsum("rs,ns->rn", picked, candid, precision=lax.Precision.HIGHEST)
    return jax.scipy.linalg.cho_solve((factor, True), right_side).T


def shards(points, omega, samples, ranks, leaf_skeleton, merge_skeleton):
    rows = points.shape[0]
    width = leaf_skeleton.shape[1]
    sub_pos = lax.axis_index("sub")
    leaf_pos = lax.axis_index("leaf")
    weights = kernel(points, lax.all_gather(points, "sub", axis=0, tiled=True)).astype(jnp.bfloat16)
    diag = jnp.dot(
        weights,
        lax.all_gather(omega, "sub", axis=0, tiled=True),
        preferred_element_type=jnp.float32,
    )
    resid = samples - diag
    live = (jnp.arange(width) < ranks[0, 0]).astype(jnp.float32)
    offsets = leaf_skeleton[0] - sub_pos * rows
    owned = ((offsets >= 0) & (offsets < rows)).astype(jnp.float32) * live
    places = jnp.clip(offsets, 0, rows - 1)
    part_rows = jnp.take(resid, places, axis=0) * owned[:, None]
    part_points = jnp.take(points, places, axis=0).astype(jnp.float32) * owned[:, None]
    omega_wide = omega.astype(jnp.float32)
    picked, chosen = lax.psum((part_rows, part_points), "sub")
    factor = factorize(picked)
    leaf_interp = interpolate(factor, resid, picked)
    local_part = jnp.einsum("nr,ns->rs", leaf_interp, omega_wide, precision=lax.Precision.HIGHEST)
    compressed = lax.psum(local_part, "sub")
    interp_levels = []
    couple_levels = []
    for height in range(1, LEVELS + 1):
        other_points, other_rows, other_comp, other_live = partner(
            (chosen, picked, compressed, live), "leaf", height - 1
        )
        coupling = (
            live[:, None]
            * other_live[None, :]
            * kernel(chosen.astype(jnp.bfloat16), other_points.astype(jnp.bfloat16))
        )
        own_new = picked - jnp.dot(coupling, other_comp, precision=lax.Precision.HIGHEST)
        other_new = other_rows - jnp.einsum(
            "ij,is->js", coupling, compressed, precision=lax.Precision.HIGHEST
        )
        is_lower = leaf_pos // 2 ** (height - 1) % 2 == 0
        cand_y = jnp.where(
            is_lower,
            jnp.concatenate([own_new, other_new], axis=0),
            jnp.concatenate([other_new, own_new], axis=0),
        )
        cand_x = jnp.where(
            is_lower,
            jnp.concatenate([chosen, other_points], axis=0),
            jnp.concatenate([other_points, chosen], axis=0),
        )
        cand_o = jnp.where(
            is_lower,
            jnp.concatenate([compressed, other_comp], axis=0),
            jnp.concatenate([other_comp, compressed], axis=0),
        )
        live = (jnp.arange(width) < ranks[0, height]).astype(jnp.float32)
        indices = merge_skeleton[0, height - 1]
        picked = jnp.take(cand_y, indices, axis=0) * live[:, None]
        chosen = jnp.take(cand_x, indices, axis=0) * live[:, None]
        factor = factorize(picked)
        node_matrix = interpolate(factor, cand_y, picked)
        compressed = jnp.einsum("nr,ns->rs", node_matrix, cand_o, precision=lax.Precision.HIGHEST)
        interp_levels.append(node_matrix)
        couple_levels.append(coupling)
    node_interp = jnp.stack(interp_levels, axis=0)[None]
    couplings = jnp.stack(couple_levels, axis=0)[None]
    return (leaf_interp, node_interp, couplings, compressed[None])


def solution(mesh):
    in_specs = (
        P(("leaf", "sub"), None),
        P(("leaf", "sub"), None),
        P(("leaf", "sub"), None),
        P("leaf", None),
        P("leaf", None),
        P("leaf", None, None),
    )
    out_specs = (
        P(("leaf", "sub"), None),
        P("leaf", None, None, None),
        P("leaf", None, None, None),
        P("leaf", None, None),
    )
    return jax.shard_map(shards, mesh=mesh, in_specs=in_specs, out_specs=out_specs, check_vma=False)
```

profile of v0, /device:TPU:16, one launch (start us, length us, event | category | flops | bytes accessed | tf_op | source)
XLA Modules:
  0.0 845.5 jit_solution(15058260484745908838)
XLA Ops:
  26.3 71.9 %all-gather.3.cloned.1.call-done = bf16[16384,64]{0,1:T(8,128)(2,1)} async-done(((bf16[256,64]{0,1:T(8,128)(2,1)}), bf16[16384,64]{0,1:T(8,128)(2,1)}) %all-gather.3.cloned.1.call-update) | async-done | bytes 2097168 | tf_op jit(solution)/shard_map/all_gather | solution.py:40
  100.3 96.8 %all-gather.5.cloned.1.call-done = bf16[16384,256]{1,0:T(8,128)(2,1)} async-done(((bf16[256,256]{1,0:T(8,128)(2,1)}), bf16[16384,256]{1,0:T(8,128)(2,1)}) %all-gather.5.cloned.1.call-update) | async-done | bytes 8388624 | tf_op jit(solution)/shard_map/all_gather | solution.py:43
  197.1 8.7 %fusion.6 = f32[256,256]{1,0:T(8,128)S(1)} fusion(f32[256,256]{1,0:T(8,128)} %param.15, bf16[16384,256]{1,0:T(8,128)(2,1)} %all-gather.5.cloned.1.call-done, bf16[256,64]{0,1:T(8,128)(2,1)} %param.13, bf16[16384,64]{0,1:T(8,128)(2,1)} %all-gather.3.cloned.1.call-done, f32[16384]{0:T(1024)S(1)} %multiply_reduce_fusion, f32[256]{0:T(256)S(1)} %multiply_reduce_fusion.11), kind=kOutput, calls=%fused_computation.24 | convolution fusion | flops 2709585920 | bytes 11109376 | tf_op jit(solution)/shard_map/dot_general | solution.py:41
  209.8 148.1 %all-reduce.5.cloned.1.call-done = f32[256,256]{1,0:T(8,128)} async-done(((f32[256,256]{1,0:T(8,128)}), f32[256,256]{1,0:T(8,128)}) %all-reduce.5.cloned.1.call-update) | async-done | bytes 262160 | tf_op jit(solution)/shard_map/psum | solution.py:54
  361.9 11.7 %cholesky.214 = f32[128,128]{1,0:T(8,128)S(1)} custom-call(f32[128,128]{1,0:T(8,128)S(1)} %cholesky.346), custom_call_target="Cholesky" | custom-call | tf_op jit(solution)/shard_map/jit(cholesky)/cholesky | solution.py:27
  373.8 9.8 %custom-call.26 = f32[1,128,128]{1,2,0:T(8,128)S(1)} custom-call(f32[1,128,128]{2,1,0:T(8,128)S(1)} %get-tuple-element.120), custom_call_target="InvertDiagBlocksLowerTriangular" | custom-call | tf_op jit(solution)/shard_map/jit(cholesky)/cholesky | solution.py:27
  384.2 11.7 %cholesky.231 = f32[128,128]{1,0:T(8,128)S(1)} custom-call(f32[128,128]{1,0:T(8,128)S(1)} %convolution_subtract_fusion.17), custom_call_target="Cholesky" | custom-call | tf_op jit(solution)/shard_map/jit(cholesky)/cholesky | solution.py:27
  402.8 19.7 %custom-call.20 = f32[2,128,128]{1,2,0:T(8,128)S(1)} custom-call(f32[2,128,128]{2,1,0:T(8,128)S(1)} %get-tuple-element.23), custom_call_target="InvertDiagBlocksLowerTriangular" | custom-call | tf_op jit(solution)/shard_map/jit(_cho_solve)/triangular_solve | solution.py:32
  429.4 148.6 %all-reduce.7.cloned.1.call-done = (f32[256,256]{1,0:T(8,128)}, f32[256,64]{1,0:T(8,128)}) async-done(((f32[256,256]{1,0:T(8,128)}, f32[256,64]{1,0:T(8,128)}), (f32[256,256]{1,0:T(8,128)}, f32[256,64]{1,0:T(8,128)})) %all-reduce.7.cloned.1.call-update) | async-done | bytes 327696 | tf_op jit(solution)/shard_map/psum | solution.py:58
  595.4 4.9 collective-permute-start.9
  611.3 11.7 %cholesky.248 = f32[128,128]{1,0:T(8,128)S(1)} custom-call(f32[128,128]{1,0:T(8,128)S(1)} %cholesky.349), custom_call_target="Cholesky" | custom-call | tf_op jit(solution)/shard_map/jit(cholesky)/cholesky | solution.py:27
  623.0 9.8 %custom-call.27 = f32[1,128,128]{1,2,0:T(8,128)S(1)} custom-call(f32[1,128,128]{2,1,0:T(8,128)S(1)} %get-tuple-element.118), custom_call_target="InvertDiagBlocksLowerTriangular" | custom-call | tf_op jit(solution)/shard_map/jit(cholesky)/cholesky | solution.py:27
  633.3 11.7 %cholesky.265 = f32[128,128]{1,0:T(8,128)S(1)} custom-call(f32[128,128]{1,0:T(8,128)S(1)} %convolution_subtract_fusion.16), custom_call_target="Cholesky" | custom-call | tf_op jit(solution)/shard_map/jit(cholesky)/cholesky | solution.py:27
  651.9 19.7 %custom-call.28 = f32[2,128,128]{1,2,0:T(8,128)S(1)} custom-call(f32[2,128,128]{2,1,0:T(8,128)S(1)} %get-tuple-element.36), custom_call_target="InvertDiagBlocksLowerTriangular" | custom-call | tf_op jit(solution)/shard_map/jit(_cho_solve)/triangular_solve | solution.py:32
  677.8 5.1 collective-permute-done.6
  685.2 4.8 collective-permute-start.11
  691.9 11.7 %cholesky.282 = f32[128,128]{1,0:T(8,128)S(1)} custom-call(f32[128,128]{1,0:T(8,128)S(1)} %cholesky.352), custom_call_target="Cholesky" | custom-call | tf_op jit(solution)/shard_map/jit(cholesky)/cholesky | solution.py:27
  703.6 9.8 %custom-call.29 = f32[1,128,128]{1,2,0:T(8,128)S(1)} custom-call(f32[1,128,128]{2,1,0:T(8,128)S(1)} %get-tuple-element.114), custom_call_target="InvertDiagBlocksLowerTriangular" | custom-call | tf_op jit(solution)/shard_map/jit(cholesky)/cholesky | solution.py:27
  713.9 11.7 %cholesky.299 = f32[128,128]{1,0:T(8,128)S(1)} custom-call(f32[128,128]{1,0:T(8,128)S(1)} %convolution_subtract_fusion.15), custom_call_target="Cholesky" | custom-call | tf_op jit(solution)/shard_map/jit(cholesky)/cholesky | solution.py:27
  732.8 19.7 %custom-call.30 = f32[2,128,128]{1,2,0:T(8,128)S(1)} custom-call(f32[2,128,128]{2,1,0:T(8,128)S(1)} %get-tuple-element.37), custom_call_target="InvertDiagBlocksLowerTriangular" | custom-call | tf_op jit(solution)/shard_map/jit(_cho_solve)/triangular_solve | solution.py:32
  771.7 11.7 %cholesky.316 = f32[128,128]{1,0:T(8,128)S(1)} custom-call(f32[128,128]{1,0:T(8,128)S(1)} %cholesky.355), custom_call_target="Cholesky" | custom-call | tf_op jit(solution)/shard_map/jit(cholesky)/cholesky | solution.py:27
  783.5 9.8 %custom-call.31 = f32[1,128,128]{1,2,0:T(8,128)S(1)} custom-call(f32[1,128,128]{2,1,0:T(8,128)S(1)} %get-tuple-element.110), custom_call_target="InvertDiagBlocksLowerTriangular" | custom-call | tf_op jit(solution)/shard_map/jit(cholesky)/cholesky | solution.py:27
  793.8 11.9 %cholesky.333 = f32[128,128]{1,0:T(8,128)S(1)} custom-call(f32[128,128]{1,0:T(8,128)S(1)} %convolution_subtract_fusion.14), custom_call_target="Cholesky" | custom-call | tf_op jit(solution)/shard_map/jit(cholesky)/cholesky | solution.py:27
  812.6 19.7 %custom-call.32 = f32[2,128,128]{1,2,0:T(8,128)S(1)} custom-call(f32[2,128,128]{2,1,0:T(8,128)S(1)} %get-tuple-element.38), custom_call_target="InvertDiagBlocksLowerTriangular" | custom-call | tf_op jit(solution)/shard_map/jit(_cho_solve)/triangular_solve | solution.py:32
  (227 shorter events, 138.2 us)
Async XLA Ops:
  7.2 91.0 %all-gather.3.cloned.1.call-start = ((), (), s32[]{:S(2)}) async-start(), calls=%async_computation | async-start | bytes 2129920 | tf_op jit(solution)/shard_map/all_gather | solution.py:40
  7.9 189.2 %all-gather.5.cloned.1.call-start = ((), (), s32[]{:S(2)}) async-start(), calls=%async_computation.1 | async-start | bytes 8519680 | tf_op jit(solution)/shard_map/all_gather | solution.py:43
  8.6 349.3 %all-reduce.5.cloned.1.call-start = ((), (), s32[]{:S(2)}) async-start(), calls=%async_computation.2 | async-start | bytes 524288 | tf_op jit(solution)/shard_map/psum | solution.py:54
  10.8 576.0 %collective-permute-start = (f32[256]{0:T(256)S(1)}, f32[256]{0:T(256)S(1)}, u32[]{:S(2)}, u32[]{:S(2)}) collective-permute-start(f32[256]{0:T(256)S(1)} %fusion.116), channel_id=1, source_target_pairs={{0,64},{64,0},{128,192},{192,128},{256,320},{320,256},{384,448},{4... | collective-permute-start | bytes 3080 | tf_op jit(solution)/shard_map/ppermute | solution.py:12
  13.3 591.5 %collective-permute-start.4 = (f32[256]{0:T(256)S(1)}, f32[256]{0:T(256)S(1)}, u32[]{:S(2)}, u32[]{:S(2)}) collective-permute-start(f32[256]{0:T(256)S(1)} %compare_convert_fusion.2), channel_id=1, source_target_pairs={{0,128},{64,192},{128,0},{192,64},{256,384},{320,448},{384,256},{4... | collective-permute-start | bytes 3080 | tf_op jit(solution)/shard_map/ppermute | solution.py:12
  17.4 666.9 %collective-permute-start.8 = (f32[256]{0:T(256)S(1)}, f32[256]{0:T(256)S(1)}, u32[]{:S(2)}, u32[]{:S(2)}) collective-permute-start(f32[256]{0:T(256)S(1)} %compare_convert_fusion.1), channel_id=1, source_target_pairs={{0,256},{64,320},{128,384},{192,448},{256,0},{320,64},{384,128},{4... | collective-permute-start | bytes 3080 | tf_op jit(solution)/shard_map/ppermute | solution.py:12
  100.3 107.7 %copy-start.2 = (bf16[256,64]{0,1:T(8,128)(2,1)S(1)}, bf16[256,64]{0,1:T(8,128)(2,1)}, u32[]{:S(2)}) copy-start(bf16[256,64]{0,1:T(8,128)(2,1)} %param.13) | copy-start | bytes 98308
  205.9 219.8 %copy-start.1 = (bf16[256,256]{1,0:T(8,128)(2,1)S(1)}, bf16[256,256]{1,0:T(8,128)(2,1)}, u32[]{:S(2)}) copy-start(bf16[256,256]{1,0:T(8,128)(2,1)} %param.14) | copy-start | bytes 393220
  207.7 370.3 %all-reduce.7.cloned.1.call-start = ((), (), s32[]{:S(2)}) async-start(), calls=%async_computation.3 | async-start | bytes 786432 | tf_op jit(solution)/shard_map/psum | solution.py:58
  357.9 69.6 %copy-start = (f32[256,256]{1,0:T(8,128)S(1)}, f32[256,256]{1,0:T(8,128)}, u32[]{:S(2)}) copy-start(f32[256,256]{1,0:T(8,128)} %all-reduce.5.cloned.1.call-done) | copy-start | bytes 786436
  427.5 162.6 %collective-permute-start.3 = (f32[256,256]{1,0:T(8,128)S(1)}, f32[256,256]{1,0:T(8,128)S(1)}, u32[]{:S(2)}, u32[]{:S(2)}) collective-permute-start(f32[256,256]{1,0:T(8,128)S(1)} %copy-done), channel_id=1, source_target_pairs={{0,64},{64,0},{128,192},{192,128},{256,320},{320,256},{384,448},{4... | collective-permute-start | bytes 786440 | tf_op jit(solution)/shard_map/ppermute | solution.py:12
  578.0 3.4 collective-permute-start.1
  581.5 21.9 %collective-permute-start.2 = (f32[256,256]{1,0:T(8,128)}, f32[256,256]{1,0:T(8,128)S(1)}, u32[]{:S(2)}, u32[]{:S(2)}) collective-permute-start(f32[256,256]{1,0:T(8,128)} %get-tuple-element.87), channel_id=1, source_target_pairs={{0,64},{64,0},{128,192},{192,128},{256,320},{320,256},{384,448},{4... | collective-permute-start | bytes 786440 | tf_op jit(solution)/shard_map/ppermute | solution.py:12
  586.7 7.7 collective-permute-start.5
  595.4 7.7 collective-permute-start.9
  600.4 73.6 %copy-start.3 = (f32[256,256]{1,0:T(8,128)S(1)}, f32[256,256]{1,0:T(8,128)}, u32[]{:S(2)}) copy-start(f32[256,256]{1,0:T(8,128)} %get-tuple-element.87) | copy-start | bytes 786436
  605.6 71.6 %collective-permute-start.7 = (f32[256,256]{1,0:T(8,128)S(1)}, f32[256,256]{1,0:T(8,128)S(1)}, u32[]{:S(2)}, u32[]{:S(2)}) collective-permute-start(f32[256,256]{1,0:T(8,128)S(1)} %get-tuple-element.96), channel_id=1, source_target_pairs={{0,128},{64,192},{128,0},{192,64},{256,384},{320,448},{384,256},{4... | collective-permute-start | bytes 786440 | tf_op jit(solution)/shard_map/ppermute | solution.py:12
  674.6 3.2 copy-start.4
  674.6 8.3 collective-permute-start.6
  682.9 2.3 copy-start.5
  685.2 75.3 %collective-permute-start.11 = (f32[256,256]{1,0:T(8,128)S(1)}, f32[256,256]{1,0:T(8,128)}, u32[]{:S(2)}, u32[]{:S(2)}) collective-permute-start(f32[256,256]{1,0:T(8,128)S(1)} %get-tuple-element.92), channel_id=1, source_target_pairs={{0,256},{64,320},{128,384},{192,448},{256,0},{320,64},{384,128},{4... | collective-permute-start | bytes 786440 | tf_op jit(solution)/shard_map/ppermute | solution.py:12
  756.7 9.9 %collective-permute-start.10 = (f32[256,256]{1,0:T(8,128)S(1)}, f32[256,256]{1,0:T(8,128)}, u32[]{:S(2)}, u32[]{:S(2)}) collective-permute-start(f32[256,256]{1,0:T(8,128)S(1)} %fusion.25), channel_id=1, source_target_pairs={{0,256},{64,320},{128,384},{192,448},{256,0},{320,64},{384,128},{4... | collective-permute-start | bytes 786440 | tf_op jit(solution)/shard_map/ppermute | solution.py:12
Sparse Core Ops, SparseCore 0:
  11.0 87.1 all-gather.2
  101.3 95.8 all-gather.4
  207.8 150.0 all-reduce.4
  426.8 151.2 all-reduce.6
where the time goes:
time: 852 us; the launch traced here: 846 us
  waiting for transfers between devices  482 us (57%)
  other arithmetic  235 us (28%)
  matrix products  38.8 us (5%)
  starting transfers between devices  38.2 us (4%)
  local copies, waits for them, and re-layouts  28.2 us (3%)
  between operations  23 us (3%)
    psum x1, waiting for transfers between devices, shards(): compressed = lax.psum(local_part, 'sub')  149 us
    psum x1, waiting for transfers between devices, shards(): picked, chosen = lax.psum((part_rows, part_points), 'sub')  148 us
    another operation x27, other arithmetic, factorize(): jnp.linalg.cholesky(gram + shift * jnp.eye(picked.shape[0], dtype=jnp.flo...  138 us
    all_gather x1, waiting for transfers between devices, shards(): lax.all_gather(omega, 'sub', axis=0, tiled=True)  96.8 us
    another operation x9, other arithmetic, interpolate(): return jax.scipy.linalg.cho_solve((factor, True), right_side).T  78.8 us
    all_gather x1, waiting for transfers between devices, shards(): lax.all_gather(points, 'sub', axis=0, tiled=True)  71.9 us
    ppermute x12, starting transfers between devices, partner(): return lax.ppermute(value, axis, pairs)  37.9 us
  transfers between devices with their start and end apart: 16, of which 9 were waited for; matrix products, arithmetic and copies ran while one was open for 27% of the time, Pallas kernels for 0%

commit v1 on v0

--- a/solution.py
+++ b/solution.py
@@ -37,7 +37,13 @@
     width = leaf_skeleton.shape[1]
     sub_pos = lax.axis_index("sub")
     leaf_pos = lax.axis_index("leaf")
-    weights = kernel(points, lax.all_gather(points, "sub", axis=0, tiled=True)).astype(jnp.bfloat16)
+    weights = kernel(
+        points,
+        jnp.concatenate(
+            lax.all_to_all(jnp.stack(lax.psum(1, axis_name="sub") * [points], axis=0), "sub", 0, 0),
+            axis=0,
+        ),
+    ).astype(jnp.bfloat16)
     diag = jnp.dot(
         weights,
         lax.all_gather(omega, "sub", axis=0, tiled=True),

time: 852 us -> 809 us (0.950)
  waiting for transfers between devices: 482 us -> 420 us
  starting transfers between devices: 38.2 us -> 54 us
    all_gather x1 -> x0, waiting for transfers between devices: 71.9 us -> none  [shards(): lax.all_gather(points, 'sub', axis=0, tiled=True)]
    all_to_all x0 -> x1, waiting for transfers between devices: none -> 34.5 us  [shards(): lax.all_to_all(jnp.stack(lax.psum(1, axis_name='sub') * [points], axis=0)...]
    all_gather x1, waiting for transfers between devices: 96.8 us -> 69.9 us  [shards(): lax.all_gather(omega, 'sub', axis=0, tiled=True)]
    all_to_all x0 -> x1, starting transfers between devices: none -> 16.5 us  [shards(): lax.all_to_all(jnp.stack(lax.psum(1, axis_name='sub') * [points], axis=0)...]
  transfers between devices with their start and end apart: 16 -> 16, of which waited for: 9 -> 10; matrix products, arithmetic and copies ran while one was open for 27% -> 21% of each run, Pallas kernels for 0% -> 0%
where the time goes in v1:
time: 809 us; the launch traced here: 802 us
  waiting for transfers between devices  420 us (52%)
  other arithmetic  234 us (29%)
  starting transfers between devices  54 us (7%)
  matrix products  36.7 us (5%)
  local copies, waits for them, and re-layouts  33.3 us (4%)
  between operations  23 us (3%)
    psum x1, waiting for transfers between devices, shards(): compressed = lax.psum(local_part, 'sub')  149 us
    psum x1, waiting for transfers between devices, shards(): picked, chosen = lax.psum((part_rows, part_points), 'sub')  148 us
    another operation x27, other arithmetic, factorize(): jnp.linalg.cholesky(gram + shift * jnp.eye(picked.shape[0], dtype=jnp.flo...  139 us
    another operation x9, other arithmetic, interpolate(): return jax.scipy.linalg.cho_solve((factor, True), right_side).T  78.8 us
    all_gather x1, waiting for transfers between devices, shards(): lax.all_gather(omega, 'sub', axis=0, tiled=True)  69.9 us
    ppermute x12, starting transfers between devices, partner(): return lax.ppermute(value, axis, pairs)  37.3 us
    all_to_all x1, waiting for transfers between devices, shards(): lax.all_to_all(jnp.stack(lax.psum(1, axis_name='sub') * [points], axis=0)...  34.5 us
    ppermute x12, waiting for transfers between devices, partner(): return lax.ppermute(value, axis, pairs)  18.2 us
  transfers between devices with their start and end apart: 16, of which 10 were waited for; matrix products, arithmetic and copies ran while one was open for 21% of the time, Pallas kernels for 0%

profile of v1, /device:TPU:16, one launch (start us, length us, event | category | flops | bytes accessed | tf_op | source)
XLA Modules:
  0.0 801.7 jit_solution(10409537255946701444)
XLA Ops:
  10.3 16.5 %all-to-all-start = ((bf16[64,256,64]{1,2,0:T(8,128)(2,1)}), bf16[64,256,64]{1,2,0:T(8,128)(2,1)S(1)}, u32[]{:S(2)}, u32[]{:S(2)}) async-start(bf16[64,256,64]{1,2,0:T(8,128)(2,1)} %stack.18), calls=%async_computation | async-start | bytes 4194304 | tf_op jit(solution)/shard_map/all_to_all | solution.py:43
  45.1 34.5 %all-to-all-done = bf16[64,256,64]{1,2,0:T(8,128)(2,1)S(1)} async-done(((bf16[64,256,64]{1,2,0:T(8,128)(2,1)}), bf16[64,256,64]{1,2,0:T(8,128)(2,1)S(1)}, u32[]{:S(2)}, u32[]{:S(2)}) %all-to-all-start) | async-done | bytes 2097184 | tf_op jit(solution)/shard_map/all_to_all | solution.py:43
  81.8 69.9 %all-gather.2.cloned.1.call-done = bf16[16384,256]{1,0:T(8,128)(2,1)} async-done(((bf16[256,256]{1,0:T(8,128)(2,1)}), bf16[16384,256]{1,0:T(8,128)(2,1)}) %all-gather.2.cloned.1.call-update) | async-done | bytes 8388624 | tf_op jit(solution)/shard_map/all_gather | solution.py:49
  151.7 8.7 %fusion.6 = f32[256,256]{1,0:T(8,128)S(1)} fusion(f32[256,256]{1,0:T(8,128)S(1)} %copy-done.9, bf16[16384,256]{1,0:T(8,128)(2,1)} %all-gather.2.cloned.1.call-done, bf16[256,64]{0,1:T(8,128)(2,1)S(1)} %copy-done.2, bf16[16384,64]{0,1:T(8,128)(2,1)} %bitcast.210, f32[16384]{0:T(1024)S(1)} %bitcast.212, f32[256]{0:T(256)S(1)} %multiply_reduce_fusion.11), kind=kOutput, calls=%fused_computation.24 | convolution fusion | flops 2709585920 | bytes 11109376 | tf_op jit(solution)/shard_map/dot_general | solution.py:47
  164.4 148.0 %all-reduce.5.cloned.1.call-done = f32[256,256]{1,0:T(8,128)} async-done(((f32[256,256]{1,0:T(8,128)}), f32[256,256]{1,0:T(8,128)}) %all-reduce.5.cloned.1.call-update) | async-done | bytes 262160 | tf_op jit(solution)/shard_map/psum | solution.py:60
  316.3 11.7 %cholesky.214 = f32[128,128]{1,0:T(8,128)S(1)} custom-call(f32[128,128]{1,0:T(8,128)S(1)} %cholesky.346), custom_call_target="Cholesky" | custom-call | tf_op jit(solution)/shard_map/jit(cholesky)/cholesky | solution.py:27
  328.1 9.8 %custom-call.26 = f32[1,128,128]{1,2,0:T(8,128)S(1)} custom-call(f32[1,128,128]{2,1,0:T(8,128)S(1)} %get-tuple-element.136), custom_call_target="InvertDiagBlocksLowerTriangular" | custom-call | tf_op jit(solution)/shard_map/jit(cholesky)/cholesky | solution.py:27
  338.4 11.7 %cholesky.231 = f32[128,128]{1,0:T(8,128)S(1)} custom-call(f32[128,128]{1,0:T(8,128)S(1)} %convolution_subtract_fusion.17), custom_call_target="Cholesky" | custom-call | tf_op jit(solution)/shard_map/jit(cholesky)/cholesky | solution.py:27
  357.2 19.7 %custom-call.20 = f32[2,128,128]{1,2,0:T(8,128)S(1)} custom-call(f32[2,128,128]{2,1,0:T(8,128)S(1)} %get-tuple-element.23), custom_call_target="InvertDiagBlocksLowerTriangular" | custom-call | tf_op jit(solution)/shard_map/jit(_cho_solve)/triangular_solve | solution.py:32
  383.8 148.6 %all-reduce.7.cloned.1.call-done = (f32[256,256]{1,0:T(8,128)}, f32[256,64]{1,0:T(8,128)}) async-done(((f32[256,256]{1,0:T(8,128)}, f32[256,64]{1,0:T(8,128)}), (f32[256,256]{1,0:T(8,128)}, f32[256,64]{1,0:T(8,128)})) %all-reduce.7.cloned.1.call-update) | async-done | bytes 327696 | tf_op jit(solution)/shard_map/psum | solution.py:64
  559.2 11.7 %cholesky.248 = f32[128,128]{1,0:T(8,128)S(1)} custom-call(f32[128,128]{1,0:T(8,128)S(1)} %cholesky.349), custom_call_target="Cholesky" | custom-call | tf_op jit(solution)/shard_map/jit(cholesky)/cholesky | solution.py:27
  570.9 9.8 %custom-call.27 = f32[1,128,128]{1,2,0:T(8,128)S(1)} custom-call(f32[1,128,128]{2,1,0:T(8,128)S(1)} %get-tuple-element.134), custom_call_target="InvertDiagBlocksLowerTriangular" | custom-call | tf_op jit(solution)/shard_map/jit(cholesky)/cholesky | solution.py:27
  581.2 11.9 %cholesky.265 = f32[128,128]{1,0:T(8,128)S(1)} custom-call(f32[128,128]{1,0:T(8,128)S(1)} %convolution_subtract_fusion.16), custom_call_target="Cholesky" | custom-call | tf_op jit(solution)/shard_map/jit(cholesky)/cholesky | solution.py:27
  599.8 19.7 %custom-call.28 = f32[2,128,128]{1,2,0:T(8,128)S(1)} custom-call(f32[2,128,128]{2,1,0:T(8,128)S(1)} %get-tuple-element.36), custom_call_target="InvertDiagBlocksLowerTriangular" | custom-call | tf_op jit(solution)/shard_map/jit(_cho_solve)/triangular_solve | solution.py:32
  628.7 4.9 collective-permute-done.6
  641.9 11.7 %cholesky.282 = f32[128,128]{1,0:T(8,128)S(1)} custom-call(f32[128,128]{1,0:T(8,128)S(1)} %cholesky.352), custom_call_target="Cholesky" | custom-call | tf_op jit(solution)/shard_map/jit(cholesky)/cholesky | solution.py:27
  653.7 9.8 %custom-call.29 = f32[1,128,128]{1,2,0:T(8,128)S(1)} custom-call(f32[1,128,128]{2,1,0:T(8,128)S(1)} %get-tuple-element.130), custom_call_target="InvertDiagBlocksLowerTriangular" | custom-call | tf_op jit(solution)/shard_map/jit(cholesky)/cholesky | solution.py:27
  664.0 12.1 %cholesky.299 = f32[128,128]{1,0:T(8,128)S(1)} custom-call(f32[128,128]{1,0:T(8,128)S(1)} %convolution_subtract_fusion.15), custom_call_target="Cholesky" | custom-call | tf_op jit(solution)/shard_map/jit(cholesky)/cholesky | solution.py:27
  678.8 5.5 while.9
  684.3 19.7 %custom-call.30 = f32[2,128,128]{1,2,0:T(8,128)S(1)} custom-call(f32[2,128,128]{2,1,0:T(8,128)S(1)} %get-tuple-element.37), custom_call_target="InvertDiagBlocksLowerTriangular" | custom-call | tf_op jit(solution)/shard_map/jit(_cho_solve)/triangular_solve | solution.py:32
  728.1 11.7 %cholesky.316 = f32[128,128]{1,0:T(8,128)S(1)} custom-call(f32[128,128]{1,0:T(8,128)S(1)} %cholesky.355), custom_call_target="Cholesky" | custom-call | tf_op jit(solution)/shard_map/jit(cholesky)/cholesky | solution.py:27
  739.9 9.8 %custom-call.31 = f32[1,128,128]{1,2,0:T(8,128)S(1)} custom-call(f32[1,128,128]{2,1,0:T(8,128)S(1)} %get-tuple-element.126), custom_call_target="InvertDiagBlocksLowerTriangular" | custom-call | tf_op jit(solution)/shard_map/jit(cholesky)/cholesky | solution.py:27
  750.2 11.9 %cholesky.333 = f32[128,128]{1,0:T(8,128)S(1)} custom-call(f32[128,128]{1,0:T(8,128)S(1)} %convolution_subtract_fusion.14), custom_call_target="Cholesky" | custom-call | tf_op jit(solution)/shard_map/jit(cholesky)/cholesky | solution.py:27
  768.8 19.7 %custom-call.32 = f32[2,128,128]{1,2,0:T(8,128)S(1)} custom-call(f32[2,128,128]{2,1,0:T(8,128)S(1)} %get-tuple-element.38), custom_call_target="InvertDiagBlocksLowerTriangular" | custom-call | tf_op jit(solution)/shard_map/jit(_cho_solve)/triangular_solve | solution.py:32
  (241 shorter events, 147.3 us)
Async XLA Ops:
  7.2 144.5 %copy-start.2 = (bf16[256,64]{0,1:T(8,128)(2,1)S(1)}, bf16[256,64]{0,1:T(8,128)(2,1)}, u32[]{:S(2)}) copy-start(bf16[256,64]{0,1:T(8,128)(2,1)} %param.13) | copy-start | bytes 98308
  7.2 144.5 %copy-start.9 = (f32[256,256]{1,0:T(8,128)S(1)}, f32[256,256]{1,0:T(8,128)}, u32[]{:S(2)}) copy-start(f32[256,256]{1,0:T(8,128)} %param.15) | copy-start | bytes 786436
  7.2 144.5 %all-gather.2.cloned.1.call-start = ((), (), s32[]{:S(2)}) async-start(), calls=%async_computation.1 | async-start | bytes 8519680 | tf_op jit(solution)/shard_map/all_gather | solution.py:49
  10.3 69.2 %all-to-all-start = ((bf16[64,256,64]{1,2,0:T(8,128)(2,1)}), bf16[64,256,64]{1,2,0:T(8,128)(2,1)S(1)}, u32[]{:S(2)}, u32[]{:S(2)}) async-start(bf16[64,256,64]{1,2,0:T(8,128)(2,1)} %stack.18), calls=%async_computation | async-start | bytes 4194304 | tf_op jit(solution)/shard_map/all_to_all | solution.py:43
  26.8 285.5 %all-reduce.5.cloned.1.call-start = ((), (), s32[]{:S(2)}) async-start(), calls=%async_computation.2 | async-start | bytes 524288 | tf_op jit(solution)/shard_map/psum | solution.py:60
  28.9 512.3 %collective-permute-start = (f32[256]{0:T(256)S(1)}, f32[256]{0:T(256)S(1)}, u32[]{:S(2)}, u32[]{:S(2)}) collective-permute-start(f32[256]{0:T(256)S(1)} %fusion.116), channel_id=1, source_target_pairs={{0,64},{64,0},{128,192},{192,128},{256,320},{320,256},{384,448},{4... | collective-permute-start | bytes 3080 | tf_op jit(solution)/shard_map/ppermute | solution.py:12
  31.5 525.0 %collective-permute-start.4 = (f32[256]{0:T(256)S(1)}, f32[256]{0:T(256)S(1)}, u32[]{:S(2)}, u32[]{:S(2)}) collective-permute-start(f32[256]{0:T(256)S(1)} %compare_convert_fusion.2), channel_id=1, source_target_pairs={{0,128},{64,192},{128,0},{192,64},{256,384},{320,448},{384,256},{4... | collective-permute-start | bytes 3080 | tf_op jit(solution)/shard_map/ppermute | solution.py:12
  35.6 603.7 %collective-permute-start.8 = (f32[256]{0:T(256)S(1)}, f32[256]{0:T(256)S(1)}, u32[]{:S(2)}, u32[]{:S(2)}) collective-permute-start(f32[256]{0:T(256)S(1)} %compare_convert_fusion.1), channel_id=1, source_target_pairs={{0,256},{64,320},{128,384},{192,448},{256,0},{320,64},{384,128},{4... | collective-permute-start | bytes 3080 | tf_op jit(solution)/shard_map/ppermute | solution.py:12
  160.4 219.6 %copy-start.1 = (bf16[256,256]{1,0:T(8,128)(2,1)S(1)}, bf16[256,256]{1,0:T(8,128)(2,1)}, u32[]{:S(2)}) copy-start(bf16[256,256]{1,0:T(8,128)(2,1)} %param.14) | copy-start | bytes 393220
  162.3 370.2 %all-reduce.7.cloned.1.call-start = ((), (), s32[]{:S(2)}) async-start(), calls=%async_computation.3 | async-start | bytes 786432 | tf_op jit(solution)/shard_map/psum | solution.py:64
  312.3 69.6 %copy-start = (f32[256,256]{1,0:T(8,128)S(1)}, f32[256,256]{1,0:T(8,128)}, u32[]{:S(2)}) copy-start(f32[256,256]{1,0:T(8,128)} %all-reduce.5.cloned.1.call-done) | copy-start | bytes 786436
  381.9 162.7 %collective-permute-start.3 = (f32[256,256]{1,0:T(8,128)S(1)}, f32[256,256]{1,0:T(8,128)S(1)}, u32[]{:S(2)}, u32[]{:S(2)}) collective-permute-start(f32[256,256]{1,0:T(8,128)S(1)} %copy-done), channel_id=1, source_target_pairs={{0,64},{64,0},{128,192},{192,128},{256,320},{320,256},{384,448},{4... | collective-permute-start | bytes 786440 | tf_op jit(solution)/shard_map/ppermute | solution.py:12
  532.5 3.4 collective-permute-start.1
  535.9 19.1 %collective-permute-start.2 = (f32[256,256]{1,0:T(8,128)}, f32[256,256]{1,0:T(8,128)S(1)}, u32[]{:S(2)}, u32[]{:S(2)}) collective-permute-start(f32[256,256]{1,0:T(8,128)} %get-tuple-element.103), channel_id=1, source_target_pairs={{0,64},{64,0},{128,192},{192,128},{256,320},{320,256},{384,448},{4... | collective-permute-start | bytes 786440 | tf_op jit(solution)/shard_map/ppermute | solution.py:12
  541.2 7.7 collective-permute-start.5
  549.6 72.3 %copy-start.3 = (f32[256,256]{1,0:T(8,128)S(1)}, f32[256,256]{1,0:T(8,128)}, u32[]{:S(2)}) copy-start(f32[256,256]{1,0:T(8,128)} %get-tuple-element.103) | copy-start | bytes 786436
  549.8 75.2 %collective-permute-start.9 = (bf16[256,64]{1,0:T(8,128)(2,1)S(1)}, bf16[256,64]{1,0:T(8,128)(2,1)S(1)}, u32[]{:S(2)}, u32[]{:S(2)}) collective-permute-start(bf16[256,64]{1,0:T(8,128)(2,1)S(1)} %get-tuple-element.106), channel_id=1, source_target_pairs={{0,256},{64,320},{128,384},{192,448},{256,0},{320,64},{384,128},{4... | collective-permute-start | bytes 98312 | tf_op jit(solution)/shard_map/ppermute | solution.py:12
  622.5 11.1 %collective-permute-start.6 = (f32[256,256]{1,0:T(8,128)S(1)}, f32[256,256]{1,0:T(8,128)S(1)}, u32[]{:S(2)}, u32[]{:S(2)}) collective-permute-start(f32[256,256]{1,0:T(8,128)S(1)} %fusion.19), channel_id=1, source_target_pairs={{0,128},{64,192},{128,0},{192,64},{256,384},{320,448},{384,256},{4... | collective-permute-start | bytes 786440 | tf_op jit(solution)/shard_map/ppermute | solution.py:12
  625.1 12.4 %collective-permute-start.7 = (f32[256,256]{1,0:T(8,128)S(1)}, f32[256,256]{1,0:T(8,128)S(1)}, u32[]{:S(2)}, u32[]{:S(2)}) collective-permute-start(f32[256,256]{1,0:T(8,128)S(1)} %get-tuple-element.112), channel_id=1, source_target_pairs={{0,128},{64,192},{128,0},{192,64},{256,384},{320,448},{384,256},{4... | collective-permute-start | bytes 786440 | tf_op jit(solution)/shard_map/ppermute | solution.py:12
  663.7 61.6 %copy-start.8 = (pred[256]{0:T(512)(128)(4,1)S(1)}, pred[256]{0:T(512)(128)(4,1)}, u32[]{:S(2)}) copy-start(pred[256]{0:T(512)(128)(4,1)} %get-tuple-element.154) | copy-start | bytes 772
  706.0 58.8 %copy-start.11 = (s32[2,2]{1,0:T(2,128)S(1)}, s32[2,2]{1,0:T(2,128)}, u32[]{:S(2)}) copy-start(s32[2,2]{1,0:T(2,128)} %get-tuple-element.383) | copy-start | bytes 52
  708.1 60.7 %copy-start.4 = (f32[256,256]{1,0:T(8,128)}, f32[256,256]{1,0:T(8,128)S(1)}, u32[]{:S(2)}) copy-start(f32[256,256]{1,0:T(8,128)S(1)} %fusion.25) | copy-start | bytes 786436
  708.1 12.6 %collective-permute-start.10 = (f32[256,256]{1,0:T(8,128)S(1)}, f32[256,256]{1,0:T(8,128)S(1)}, u32[]{:S(2)}, u32[]{:S(2)}) collective-permute-start(f32[256,256]{1,0:T(8,128)S(1)} %fusion.25), channel_id=1, source_target_pairs={{0,256},{64,320},{128,384},{192,448},{256,0},{320,64},{384,128},{4... | collective-permute-start | bytes 786440 | tf_op jit(solution)/shard_map/ppermute | solution.py:12
  710.9 12.7 %collective-permute-start.11 = (f32[256,256]{1,0:T(8,128)S(1)}, f32[256,256]{1,0:T(8,128)S(1)}, u32[]{:S(2)}, u32[]{:S(2)}) collective-permute-start(f32[256,256]{1,0:T(8,128)S(1)} %get-tuple-element.108), channel_id=1, source_target_pairs={{0,256},{64,320},{128,384},{192,448},{256,0},{320,64},{384,128},{4... | collective-permute-start | bytes 786440 | tf_op jit(solution)/shard_map/ppermute | solution.py:12
  (4 other events, 73.8 us)
Sparse Core Ops, SparseCore 0:
  11.1 140.5 all-gather.1
  162.4 149.8 all-reduce.4
  381.2 151.2 all-reduce.6
